TPU v7x, 32 devices: a whole 2x2x4 slice. The times are simulated.
32 devices in a mesh: grp: 2 (over x), ctx: 16 (over z, y, core).
Axes of the slice: x: 2, y: 2, z: 4, core: 2. Of those that a mesh axis runs over, the one named last changes fastest.
Arguments:
- query_series: bfloat16 [4096, 2048], P(('grp', 'ctx')), parts along dimension 0, may hold values from -6 to 6
- key_series: bfloat16 [4096, 2048], P(('grp', 'ctx')), parts along dimension 0, may hold values from -6 to 6
- value_series: bfloat16 [4096, 2048], P(('grp', 'ctx')), parts along dimension 0, may hold values from -6 to 6
- grad_out: bfloat16 [4096, 2048], P(('grp', 'ctx')), parts along dimension 0, may hold values from -6 to 6
- gate_mask: int32 [4096], P(('grp', 'ctx')), parts along dimension 0, may hold values 0 or 1
- filter_spectrum: float32 [2, 32, 128, 2048], P(None, 'ctx'), may hold values from -6 to 6
Outputs:
- mixer_out: bfloat16 [4096, 2048], P(('grp', 'ctx')), parts along dimension 0
- grad_queries: bfloat16 [4096, 2048], P(('grp', 'ctx')), parts along dimension 0
- grad_keys: bfloat16 [4096, 2048], P(('grp', 'ctx')), parts along dimension 0
- grad_values: bfloat16 [4096, 2048], P(('grp', 'ctx')), parts along dimension 0
- grad_spectrum: float32 [2, 64, 128, 2048], P(None, ('grp', 'ctx')), parts along dimension 1
There are 2 independent parts, one for each index of `grp`. A program takes and returns all parts, laid end to end along the dimension named above; an argument that names none is the same for every part. Nothing has to cross between parts.
All inputs are finite; a program needn't handle non-finite values. No bound on the sum of `gate_mask` on one device may be relied on, other than what follows from the above.
Results may differ from a plain program's by a relative error of at most 0.0051.
Values may be sent and summed in bfloat16 or wider, within the bound.
A program may use at most 128 MiB of HBM per device.

v0:
```python
import math

import jax
import jax.numpy as jnp
import numpy as np
from jax import lax
from jax.sharding import PartitionSpec as P

highest = lax.Precision.HIGHEST


def class_order(devices):
    indices = np.arange(2 * devices)
    pair_index = indices // 2
    parity = indices % 2
    return np.where(
        pair_index == 0,
        parity * devices,
        np.where(parity == 0, pair_index, 2 * devices - pair_index),
    )


def partner(spectrum):
    flipped = jnp.flip(spectrum, axis=-2)
    crossed = jnp.flip(flipped, axis=-3)
    anchor_head = jnp.roll(flipped[..., 0:1, :, :], 1, axis=-2)
    anchor = jnp.concatenate([anchor_head, flipped[..., 1:2, :, :]], axis=-3)
    return jnp.where(lax.axis_index("ctx") == 0, anchor, crossed)


def forward_spectra(series):
    devices = lax.axis_size("ctx")
    tok_rows = series.shape[1]
    group_rows = tok_rows // devices
    classes = 2 * devices
    fft_length = classes * tok_rows
    ordering = class_order(devices)
    norm_factor = 1.0 / math.sqrt(fft_length)
    positions = lax.axis_index("ctx") * group_rows + jnp.arange(group_rows, dtype=jnp.int32)
    offsets = jnp.arange(devices, dtype=jnp.int32) * tok_rows
    order_column = jnp.asarray(ordering, jnp.int32)[:, None, None]
    first_turns = order_column * (offsets[None, :, None] + positions[None, None, :]) % fft_length
    first_angle = first_turns.astype(jnp.float32) * (-2.0 * math.pi / fft_length)
    first_table = jnp.stack([jnp.cos(first_angle), jnp.sin(first_angle)])
    rows_index = np.arange(tok_rows)
    second_angle = 2.0 * np.pi * (np.outer(rows_index, rows_index) % tok_rows) / tok_rows
    cos_second = np.cos(second_angle)
    sin_second = -np.sin(second_angle)
    row_real = np.stack([cos_second, -sin_second], axis=1)
    row_imag = np.stack([sin_second, cos_second], axis=1)
    second_table = jnp.asarray(np.stack([row_real, row_imag]) * norm_factor, jnp.float32)
    shaped = series.reshape(2, devices, group_rows, series.shape[-1])
    received = lax.all_to_all(shaped, "ctx", split_axis=1, concat_axis=1, tiled=True)
    channels = received.shape[-1]
    widened = received.astype(jnp.float32)
    parts = jnp.einsum("qjab,sabx->sqjbx", first_table, widened, precision=highest)
    parts = jnp.stack([parts[0, 0] - parts[1, 1], parts[0, 1] + parts[1, 0]])[None]
    signals = parts.shape[0]
    stacked = parts.reshape(signals * 2, devices, 2, group_rows, channels)
    received = lax.all_to_all(stacked, "ctx", split_axis=1, concat_axis=3, tiled=True)
    channels = received.shape[-1]
    signals = received.shape[0] // 2
    shaped = received.reshape(signals, 2, 2, tok_rows, channels)
    joined = jnp.einsum("qdpb,speby->sqedy", second_table, shaped, precision=highest)
    spectrum = joined.reshape(signals * 2, 2, tok_rows, channels)
    return spectrum.reshape(spectrum.shape[0] // 2, 2, 2, tok_rows, series.shape[-1])


def inverse_series(spectra):
    devices = lax.axis_size("ctx")
    signals = spectra.shape[0]
    tok_rows = spectra.shape[3]
    channels_all = spectra.shape[4]
    group_rows = tok_rows // devices
    classes = 2 * devices
    fft_length = classes * tok_rows
    ordering = class_order(devices)
    norm_factor = 1.0 / math.sqrt(fft_length)
    location = lax.axis_index("ctx")
    own_classes = jnp.stack(
        [
            jnp.where(location == 0, 0, location),
            jnp.where(location == 0, devices, classes - location),
        ]
    )
    rows_index = jnp.arange(tok_rows, dtype=jnp.int32)
    square_turns = rows_index[:, None] * rows_index[None, :] * classes % fft_length
    second_turns = (
        square_turns[None, :, :] + own_classes[:, None, None] * rows_index[None, :, None]
    ) % fft_length
    second_angle = second_turns.astype(jnp.float32) * (2.0 * math.pi / fft_length)
    cos_second = jnp.cos(second_angle)
    sin_second = jnp.sin(second_angle)
    second_table = jnp.stack(
        [jnp.stack([cos_second, -sin_second], axis=2), jnp.stack([sin_second, cos_second], axis=2)],
        axis=1,
    )
    stacked = jnp.einsum("eqbpd,spedy->sqeby", second_table, spectra, precision=highest)
    stacked = stacked.reshape(signals * 2, 1, 2, tok_rows, channels_all)
    first_angle = 2.0 * np.pi * (np.outer(np.arange(devices), ordering) % classes) / classes
    cos_first = np.cos(first_angle)
    sin_first = np.sin(first_angle)
    full_table = (
        np.stack(
            [np.stack([cos_first, -sin_first], axis=1), np.stack([sin_first, cos_first], axis=1)]
        )
        * norm_factor
    )
    first_table = jnp.asarray(full_table, jnp.float32)
    received = lax.all_to_all(stacked, "ctx", split_axis=3, concat_axis=1, tiled=True)
    channels = received.shape[-1]
    flattened = received.reshape(signals, 2, classes, group_rows * channels)
    time_series = jnp.einsum("qapj,spjx->sqax", first_table, flattened, precision=highest)
    time_series = time_series.reshape(2, devices, group_rows, channels)
    outputs = lax.all_to_all(time_series, "ctx", split_axis=1, concat_axis=1, tiled=True)
    return outputs.reshape(2, tok_rows, channels_all)


def shards(query_series, key_series, value_series, grad_out, gate_mask, filter_spectrum):
    gating = gate_mask.astype(jnp.float32)[:, None]
    gated_pair = (
        gating * key_series.astype(jnp.float32) * value_series.astype(jnp.float32)
    ).astype(jnp.bfloat16)
    back_signal = (query_series.astype(jnp.float32) * grad_out.astype(jnp.float32)).astype(
        jnp.bfloat16
    )
    series = jnp.stack([gated_pair, back_signal])
    filter_real = filter_spectrum[0]
    filter_imag = filter_spectrum[1]
    combined = forward_spectra(series)[0]
    mirror = partner(combined)
    signal_real = 0.5 * (combined[0] + mirror[0])
    signal_imag = 0.5 * (combined[1] - mirror[1])
    adjoint_real = 0.5 * (combined[1] + mirror[1])
    adjoint_imag = 0.5 * (mirror[0] - combined[0])
    conv_real = signal_real * filter_real - signal_imag * filter_imag
    conv_imag = signal_real * filter_imag + signal_imag * filter_real
    back_real = adjoint_real * filter_real + adjoint_imag * filter_imag
    back_imag = adjoint_imag * filter_real - adjoint_real * filter_imag
    grad_spectrum = jnp.stack(
        [
            adjoint_real * signal_real + adjoint_imag * signal_imag,
            adjoint_imag * signal_real - adjoint_real * signal_imag,
        ]
    )
    minus_pair = jnp.stack([conv_real + back_imag, conv_imag - back_real])
    mirror_back = partner(minus_pair)
    joined = jnp.stack(
        [
            0.5 * (conv_real - back_imag + mirror_back[0]),
            0.5 * (conv_imag + back_real - mirror_back[1]),
        ]
    )
    outputs = inverse_series(joined[None])
    conv_out = outputs[0]
    grad_mixed = outputs[1]
    mixer_out = (query_series.astype(jnp.float32) * conv_out).astype(jnp.bfloat16)
    grad_queries = (grad_out.astype(jnp.float32) * conv_out).astype(jnp.bfloat16)
    grad_keys = (grad_mixed * gating * value_series.astype(jnp.float32)).astype(jnp.bfloat16)
    grad_values = (grad_mixed * gating * key_series.astype(jnp.float32)).astype(jnp.bfloat16)
    return (mixer_out, grad_queries, grad_keys, grad_values, grad_spectrum)


def solution(mesh):
    placed = (
        P(("grp", "ctx"), None),
        P(("grp", "ctx"), None),
        P(("grp", "ctx"), None),
        P(("grp", "ctx"), None),
        P(("grp", "ctx")),
        P(None, "ctx", None, None),
    )
    return jax.shard_map(
        shards,
        mesh=mesh,
        in_specs=placed,
        out_specs=(
            P(("grp", "ctx"), None),
            P(("grp", "ctx"), None),
            P(("grp", "ctx"), None),
            P(("grp", "ctx"), None),
            P(None, ("grp", "ctx"), None, None),
        ),
        check_vma=False,
    )
```

profile of v0, /device:TPU:13, one launch (start us, length us, event | category | flops | bytes accessed | tf_op | source)
XLA Modules:
  0.0 509.6 jit_solution(8344288658746940841)
XLA Ops:
  5.4 6.6 %all-to-all-start = ((bf16[2,16,8,2048]{3,0,2,1:T(2,128)(2,1)}), bf16[2,16,8,2048]{3,0,2,1:T(2,128)(2,1)S(1)}, u32[]{:S(2)}, u32[]{:S(2)}) async-start(bf16[2,16,8,2048]{3,0,2,1:T(2,128)(2,1)} %copy.28), calls=%async_computation | async-start | bytes 2097152 | tf_op jit(solution)/shard_map/all_to_all | solution.py:53
  12.4 24.4 %all-to-all-done = bf16[2,16,8,2048]{3,0,2,1:T(2,128)(2,1)S(1)} async-done(((bf16[2,16,8,2048]{3,0,2,1:T(2,128)(2,1)}), bf16[2,16,8,2048]{3,0,2,1:T(2,128)(2,1)S(1)}, u32[]{:S(2)}, u32[]{:S(2)}) %all-to-all-start) | async-done | bytes 1048608 | tf_op jit(solution)/shard_map/all_to_all | solution.py:53
  48.1 4.4 pad_maximum_fusion.1
  52.4 3.9 copy.50
  56.4 5.1 all-to-all-start.1
  62.3 91.6 %all-to-all-done.1 = f32[2,16,2,8,2048]{4,2,3,0,1:T(2,128)} async-done(((f32[2,16,2,8,2048]{4,2,3,0,1:T(2,128)}), f32[2,16,2,8,2048]{4,2,3,0,1:T(2,128)}, u32[]{:S(2)}, u32[]{:S(2)}) %all-to-all-start.1) | async-done | bytes 4194336 | tf_op jit(solution)/shard_map/all_to_all | solution.py:60
  153.9 7.2 %fusion.5 = f32[1,2,2,128,2048]{4,3,1,2,0:T(8,128)S(1)} fusion(f32[2,128,2,128,1]{3,1,2,0,4:T(8,128)S(1)} %copy-done.10, f32[2,1,2,16,8,2048]{5,2,4,0,3,1:T(2,128)} %bitcast.7), kind=kOutput, calls=%fused_computation.19 | convolution fusion | flops 3221225472 | bytes 8650752 | tf_op jit(solution)/shard_map/qdpb,speby->sqedy/dot_general | solution.py:64
  164.5 32.7 %rev.10 = f32[2,2,128,2048]{3,2,1,0:T(8,128)} reverse(f32[2,2,128,2048]{3,2,1,0:T(8,128)} %bitcast.113), dimensions={1,2} | reverse | bytes 8388608 | tf_op jit(solution)/shard_map/jit(_flip)/rev | solution.py:25
  202.1 13.7 %slice.101 = f32[2,1,128,2048]{3,2,1,0:T(8,128)S(1)} reverse(f32[2,1,128,2048]{3,2,1,0:T(8,128)} %slice.123), dimensions={2} | reverse | bytes 4194304 | tf_op jit(solution)/shard_map/slice | solution.py:27
  215.8 16.8 %slice.99 = f32[2,1,127,2048]{3,2,1,0:T(8,128)} reverse(f32[2,1,127,2048]{3,2,1,0:T(8,128)} %slice.122), dimensions={2} | reverse | bytes 4161536 | tf_op jit(solution)/shard_map/jit(_roll_static)/slice | solution.py:26
  232.6 3.9 maximum_select_fusion
  241.6 6.9 %fusion.45 = (f32[1,2,128,2048]{3,2,1,0:T(8,128)S(1)}, f32[1,2,128,2048]{3,2,1,0:T(8,128)}, f32[1,2,128,2048]{3,2,1,0:T(8,128)}, f32[1,2,128,2048]{3,2,1,0:T(8,1...) fusion(f32[1,2,128,2048]{3,2,1,0:T(8,128)S(1)} %get-tuple-element.6, ...), kind=kLoop, calls=%fused_computation.103 | loop fusion | flops 8912896 | bytes 27262976 | tf_op jit(solution)/shard_map/add | solution.py:146
  253.7 14.0 %slice.109 = f32[2,1,127,2048]{3,2,1,0:T(8,128)S(1)} reverse(f32[2,1,127,2048]{3,2,1,0:T(8,128)} %fusion.11), dimensions={2} | reverse | bytes 4161536 | tf_op jit(solution)/shard_map/jit(_roll_static)/slice | solution.py:26
  267.7 16.7 %slice.111 = f32[2,1,128,2048]{3,2,1,0:T(8,128)} reverse(f32[2,1,128,2048]{3,2,1,0:T(8,128)} %fusion.12), dimensions={2} | reverse | bytes 4194304 | tf_op jit(solution)/shard_map/slice | solution.py:27
  284.4 32.6 %rev.11 = f32[2,2,128,2048]{3,2,1,0:T(8,128)} reverse(f32[2,2,128,2048]{3,2,1,0:T(8,128)} %pad_maximum_fusion), dimensions={1,2} | reverse | bytes 8388608 | tf_op jit(solution)/shard_map/jit(_flip)/rev | solution.py:25
  317.1 3.9 maximum_select_fusion.1
  324.1 8.8 %fusion.8 = f32[2,1,2,128,2048]{3,4,0,2,1:T(8,128)} fusion(f32[2,1,128,2,128]{4,2,3,1,0:T(8,128)S(1)} %get-tuple-element.31, f32[2,1,128,2,128]{4,2,3,1,0:T(8,128)S(1)} %get-tuple-element.30, f32[1,2,128,2048]{3,2,1,0:T(8,128)S(1)} %get-tuple-element.23, f32[1,2,128,2048]{3,2,1,0:T(8,128)S(1)} %get-tuple-element.22), kind=kOutput, calls=%fused_computation.20 | convolution fusion | flops 3222405120 | bytes 8912896 | tf_op jit(solution)/shard_map/eqbpd,spedy->sqeby/dot_general | solution.py:98
  333.0 7.3 %copy.37 = f32[2,1,2,128,2048]{4,0,2,1,3:T(2,128)} copy(f32[2,1,2,128,2048]{3,4,0,2,1:T(8,128)} %fusion.8) | data formatting | bytes 8388608 | tf_op jit(solution)/shard_map/reshape | solution.py:99
  340.3 97.2 %all_to_all.40 = f32[2,1,2,128,2048]{4,0,2,1,3:T(2,128)S(1)} all-to-all(f32[2,1,2,128,2048]{4,0,2,1,3:T(2,128)} %copy.37), channel_id=1, replica_groups=mesh['grp'=2,'ctx'=16] {'ctx'}, dimensions={3} | all-to-all | bytes 8388608 | tf_op jit(solution)/shard_map/all_to_all | solution.py:110
  442.1 4.9 reshape.302
  447.1 4.1 fusion.48
  453.9 5.3 %all-to-all-start.3 = ((f32[2,16,8,2048]{3,2,0,1:T(8,128)}), f32[2,16,8,2048]{3,2,0,1:T(8,128)S(1)}, u32[]{:S(2)}, u32[]{:S(2)}) async-start(f32[2,16,8,2048]{3,2,0,1:T(8,128)} %copy.40), calls=%async_computation.3 | async-start | bytes 4194304 | tf_op jit(solution)/shard_map/all_to_all | solution.py:115
  459.2 4.8 pad_maximum_fusion.2
  464.0 42.6 %all-to-all-done.3 = f32[2,16,8,2048]{3,2,0,1:T(8,128)S(1)} async-done(((f32[2,16,8,2048]{3,2,0,1:T(8,128)}), f32[2,16,8,2048]{3,2,0,1:T(8,128)S(1)}, u32[]{:S(2)}, u32[]{:S(2)}) %all-to-all-start.3) | async-done | bytes 2097184 | tf_op jit(solution)/shard_map/all_to_all | solution.py:115
  (58 shorter events, 49.3 us)
Async XLA Ops:
  3.3 8.7 %copy-start.12 = (s32[32]{0:T(128)S(1)}, s32[32]{0:T(128)}, u32[]{:S(2)}) copy-start(s32[32]{0:T(128)} %constant.57.clone) | copy-start | bytes 388
  5.4 31.4 %all-to-all-start = ((bf16[2,16,8,2048]{3,0,2,1:T(2,128)(2,1)}), bf16[2,16,8,2048]{3,0,2,1:T(2,128)(2,1)S(1)}, u32[]{:S(2)}, u32[]{:S(2)}) async-start(bf16[2,16,8,2048]{3,0,2,1:T(2,128)(2,1)} %copy.28), calls=%async_computation | async-start | bytes 2097152 | tf_op jit(solution)/shard_map/all_to_all | solution.py:53
  56.4 97.5 %copy-start.10 = (f32[2,128,2,128,1]{3,1,2,0,4:T(8,128)S(1)}, f32[2,128,2,128,1]{3,1,2,0,4:T(8,128)}, u32[]{:S(2)}) copy-start(f32[2,128,2,128,1]{3,1,2,0,4:T(8,128)} %constant.61) | copy-start | bytes 786436
  56.4 97.5 %all-to-all-start.1 = ((f32[2,16,2,8,2048]{4,2,3,0,1:T(2,128)}), f32[2,16,2,8,2048]{4,2,3,0,1:T(2,128)}, u32[]{:S(2)}, u32[]{:S(2)}) async-start(f32[2,16,2,8,2048]{4,2,3,0,1:T(2,128)} %copy.50), calls=%async_computation.1 | async-start | bytes 8388608 | tf_op jit(solution)/shard_map/all_to_all | solution.py:60
  161.2 3.3 copy-start.2
  197.2 3.3 copy-start
  232.6 4.1 copy-start.1
  232.6 5.3 %copy-start.3 = (f32[1,2,2,128,2048]{4,3,1,2,0:T(8,128)S(1)}, f32[1,2,2,128,2048]{4,3,1,2,0:T(8,128)}, u32[]{:S(2)}) copy-start(f32[1,2,2,128,2048]{4,3,1,2,0:T(8,128)} %copy-done.2) | copy-start | bytes 12582916
  317.0 3.9 copy-start.4
  317.0 4.1 copy-start.5
  317.0 4.7 copy-start.6
  317.0 5.3 %copy-start.7 = (f32[1,2,128,2048]{3,2,1,0:T(8,128)S(1)}, f32[1,2,128,2048]{3,2,1,0:T(8,128)}, u32[]{:S(2)}) copy-start(f32[1,2,128,2048]{3,2,1,0:T(8,128)} %get-tuple-element.18) | copy-start | bytes 6291460
  442.1 4.9 copy-start.11
  453.9 52.7 %all-to-all-start.3 = ((f32[2,16,8,2048]{3,2,0,1:T(8,128)}), f32[2,16,8,2048]{3,2,0,1:T(8,128)S(1)}, u32[]{:S(2)}, u32[]{:S(2)}) async-start(f32[2,16,8,2048]{3,2,0,1:T(8,128)} %copy.40), calls=%async_computation.3 | async-start | bytes 4194304 | tf_op jit(solution)/shard_map/all_to_all | solution.py:115
  459.2 47.4 %copy-start.8 = (bf16[128,2048]{1,0:T(8,128)(2,1)S(1)}, bf16[128,2048]{1,0:T(8,128)(2,1)}, u32[]{:S(2)}) copy-start(bf16[128,2048]{1,0:T(8,128)(2,1)} %param.10) | copy-start | bytes 1572868
  459.2 47.4 %copy-start.9 = (bf16[128,2048]{1,0:T(8,128)(2,1)S(1)}, bf16[128,2048]{1,0:T(8,128)(2,1)}, u32[]{:S(2)}) copy-start(bf16[128,2048]{1,0:T(8,128)(2,1)} %param.12) | copy-start | bytes 1572868
where the time goes:
time: 519 us; the launch traced here: 510 us
  local copies, waits for them, and re-layouts  169 us (33%)
  waiting for transfers between devices  159 us (31%)
  blocking collectives  97.2 us (19%)
  other arithmetic  43.6 us (8%)
  matrix products  23.7 us (5%)
  starting transfers between devices  16.9 us (3%)
    all_to_all x1, blocking collectives, inverse_series(): lax.all_to_all(stacked, 'ctx', split_axis=3, concat_axis=1, tiled=True)  97.2 us
    all_to_all x1, waiting for transfers between devices, forward_spectra(): lax.all_to_all(stacked, 'ctx', split_axis=1, concat_axis=3, tiled=True)  91.6 us
    rev x2, local copies, waits for them, and re-layouts, partner(): crossed = jnp.flip(flipped, axis=-3)  65.3 us
    all_to_all x1, waiting for transfers between devices, inverse_series(): lax.all_to_all(time_series, 'ctx', split_axis=1, concat_axis=1, tiled=True)  42.6 us
    slice x3, local copies, waits for them, and re-layouts, partner(): anchor = jnp.concatenate([anchor_head, flipped[..., 1:2, :, :]], axis=-3)  33.7 us
    slice x4, local copies, waits for them, and re-layouts, partner(): anchor_head = jnp.roll(flipped[..., 0:1, :, :], 1, axis=-2)  32.4 us
    all_to_all x1, waiting for transfers between devices, forward_spectra(): lax.all_to_all(shaped, 'ctx', split_axis=1, concat_axis=1, tiled=True)  24.4 us
  transfers between devices with their start and end apart: 3, of which 3 were waited for; matrix products, arithmetic and copies ran while one was open for 1% of the time, Pallas kernels for 0%

commit v1 on v0

--- a/solution.py
+++ b/solution.py
@@ -1,9 +1,12 @@
+import functools
 import math
 
 import jax
 import jax.numpy as jnp
 import numpy as np
 from jax import lax
+from jax.experimental import pallas as pl
+from jax.experimental.pallas import tpu as pltpu
 from jax.sharding import PartitionSpec as P
 
 highest = lax.Precision.HIGHEST
@@ -116,7 +119,7 @@
     return outputs.reshape(2, tok_rows, channels_all)
 
 
-def shards(query_series, key_series, value_series, grad_out, gate_mask, filter_spectrum):
+def narrow_shards(query_series, key_series, value_series, grad_out, gate_mask, filter_spectrum):
     gating = gate_mask.astype(jnp.float32)[:, None]
     gated_pair = (
         gating * key_series.astype(jnp.float32) * value_series.astype(jnp.float32)
@@ -161,6 +164,381 @@
     return (mixer_out, grad_queries, grad_keys, grad_values, grad_spectrum)
 
 
+SUB = 16
+LANES = 128
+
+
+def split_table(values):
+    exact = np.asarray(values, np.float32)
+    high = exact.astype(jnp.bfloat16)
+    low = (exact - high.astype(np.float32)).astype(jnp.bfloat16)
+    return np.stack([high, low], axis=-3)
+
+
+def device_tables(devices):
+    classes = 2 * devices
+    turns = 2.0 * np.pi * (np.outer(np.arange(devices), np.arange(devices)) % classes) / classes
+    small = np.stack([np.cos(turns), -np.sin(turns)], axis=1)
+    small[0, 1] = np.where(np.arange(devices) % 2 == 0, 1.0, -1.0)
+    small = small.reshape(classes, devices)
+    full = np.kron(small, np.eye(SUB))
+    return split_table(full), split_table(full.T)
+
+
+def row_tables(devices, rows):
+    classes = 2 * devices
+    length = classes * rows
+    half = rows // 2
+    place = np.arange(rows)
+    tables = np.zeros((devices, 2, rows, 2, rows))
+    for group in range(1, devices):
+        freq = group + classes * place
+        angle = 2.0 * np.pi * (np.outer(freq, place) % length) / length
+        tables[group, 0, :, 0] = np.cos(angle)
+        tables[group, 0, :, 1] = np.sin(angle)
+        tables[group, 1, :, 0] = -np.sin(angle)
+        tables[group, 1, :, 1] = np.cos(angle)
+    for part, first in ((0, 0), (1, devices)):
+        freq = first + classes * np.arange(half)
+        angle = 2.0 * np.pi * (np.outer(freq, place) % length) / length
+        tables[0, 0, part * half : (part + 1) * half, part] = np.cos(angle)
+        tables[0, 1, part * half : (part + 1) * half, part] = -np.sin(angle)
+    tables[0, 1, 0, 0] = np.where(place % 2 == 0, 1.0, -1.0)
+    tables = tables.reshape(devices, 2 * rows, 2 * rows) / math.sqrt(length)
+    return split_table(tables), split_table(tables.transpose(0, 2, 1))
+
+
+def fold_tables(rows):
+    half = rows // 2
+    fold = np.zeros((2, 2, rows, 2, 2, rows))
+    spread = np.zeros((2, 2, 2, rows, 2, rows))
+    for d in range(rows):
+        for part, sign in ((0, 1.0), (1, -1.0)):
+            fold[1, part, d, part, 0, d] = 1.0
+            fold[1, part, d, part, 1, rows - 1 - d] = sign
+            spread[1, part, 0, d, part, d] = 1.0
+            spread[1, part, 1, rows - 1 - d, part, d] = sign
+    for d in range(half):
+        for part, sign in ((0, 1.0), (1, -1.0)):
+            if d > 0:
+                fold[0, part, d, part, 0, d] = 1.0
+                fold[0, part, d, part, 0, rows - d] = sign
+                spread[0, part, 0, d, part, d] = 1.0
+                spread[0, part, 0, rows - d, part, d] = sign
+            fold[0, part, half + d, part, 1, d] = 1.0
+            fold[0, part, half + d, part, 1, rows - 1 - d] = sign
+            spread[0, part, 1, d, part, half + d] = 1.0
+            spread[0, part, 1, rows - 1 - d, part, half + d] = sign
+    fold[0, 0, 0, 0, 0, 0] = 1.0
+    fold[0, 1, 0, 0, 0, half] = 1.0
+    spread[0, 0, 0, 0, 0, 0] = 1.0
+    spread[0, 0, 0, half, 1, 0] = 1.0
+    return (
+        fold.reshape(2, 2 * rows, 4 * rows).astype(jnp.bfloat16),
+        spread.reshape(2, 4 * rows, 2 * rows).astype(jnp.bfloat16),
+    )
+
+
+def dot(left, right):
+    return jnp.dot(left, right, preferred_element_type=jnp.float32)
+
+
+def exchange_kernel(
+    devices,
+    rows,
+    width,
+    query_ref,
+    key_ref,
+    value_ref,
+    grad_ref,
+    gate_ref,
+    filter_ref,
+    fold_ref,
+    mix_ref,
+    unmix_ref,
+    table_ref,
+    back_ref,
+    got_grad,
+    got_series,
+    send_signal,
+    got_signal,
+    send_filter,
+    got_filter,
+    mixed,
+    turned,
+    send_grad,
+    send_series,
+    send_sems,
+    recv_sems,
+    local_sems,
+):
+    me = lax.axis_index("ctx")
+    barrier = pltpu.get_barrier_semaphore()
+
+    def greet(step, _):
+        pl.semaphore_signal(
+            barrier,
+            inc=1,
+            device_id={"ctx": lax.rem(me + step, devices)},
+            device_id_type=pl.DeviceIdType.MESH,
+        )
+        return 0
+
+    lax.fori_loop(1, devices, greet, 0)
+
+    def remote(kind, source, target, step_from, to):
+        return pltpu.make_async_remote_copy(
+            src_ref=source.at[to],
+            dst_ref=target.at[step_from],
+            send_sem=send_sems.at[kind, to],
+            recv_sem=recv_sems.at[kind, step_from],
+            device_id={"ctx": to},
+            device_id_type=pl.DeviceIdType.MESH,
+        )
+
+    def start_all(kind, source, target):
+        def body(step, _):
+            remote(kind, source, target, me, lax.rem(me + step, devices)).start()
+            return 0
+
+        lax.fori_loop(1, devices, body, 0)
+
+    def wait_received(kind, source, target, first=1):
+        def body(step, _):
+            other = lax.rem(me + devices - step, devices)
+            remote(kind, source, target, other, other).wait_recv()
+            return 0
+
+        lax.fori_loop(first, devices, body, 0)
+
+    def wait_sent(kind, source, target):
+        def body(step, _):
+            remote(kind, source, target, me, lax.rem(me + step, devices)).wait_send()
+            return 0
+
+        lax.fori_loop(1, devices, body, 0)
+
+    gating = gate_ref[...]
+    for to in range(devices):
+        span = slice(to * width, (to + 1) * width)
+        gated = gating * key_ref[:, span].astype(jnp.float32) * value_ref[:, span].astype(jnp.float32)
+        back = query_ref[:, span].astype(jnp.float32) * grad_ref[:, span].astype(jnp.float32)
+        send_signal[to, 0] = gated.astype(jnp.bfloat16)
+        send_signal[to, 1] = back.astype(jnp.bfloat16)
+    pl.semaphore_wait(barrier, devices - 1)
+    start_all(0, send_signal, got_signal)
+    got_signal[me] = send_signal[me]
+
+    for to in range(devices):
+        span = slice(to * width, (to + 1) * width)
+        block = filter_ref[:, span]
+        high = block.astype(jnp.bfloat16)
+        low = (block - high.astype(jnp.float32)).astype(jnp.bfloat16)
+        folded = dot(fold_ref[...], high) + dot(fold_ref[...], low)
+        send_filter[to] = folded.astype(jnp.bfloat16)
+    start_all(1, send_filter, got_filter)
+    got_filter[me] = send_filter[me]
+
+    wait_received(0, send_signal, got_signal)
+
+    def mix(part, _):
+        span = pl.ds(pl.multiple_of(part * SUB, SUB), SUB)
+        columns = jnp.concatenate(
+            [got_signal[:, which, span, :].reshape(devices * SUB, width) for which in (0, 1)], axis=1
+        )
+        result = dot(mix_ref[0], columns) + dot(mix_ref[1], columns)
+        mixed[:, span, :] = result.astype(jnp.bfloat16).reshape(2 * devices, SUB, 2 * width)
+        return 0
+
+    lax.fori_loop(0, rows // SUB, mix, 0)
+    wait_received(1, send_filter, got_filter)
+
+    row_index = lax.broadcasted_iota(jnp.int32, (rows, width), 0)
+
+    def one_group(group, _):
+        source = mixed[pl.ds(2 * group, 2)].reshape(2 * rows, 2 * width)
+        spectra = dot(table_ref[group, 0], source) + dot(table_ref[group, 1], source)
+        signal_real = spectra[:rows, :width]
+        signal_imag = spectra[rows:, :width]
+        adjoint_real = spectra[:rows, width:]
+        adjoint_imag = spectra[rows:, width:]
+        response = got_filter[group].astype(jnp.float32)
+        filter_real = response[:rows]
+        filter_imag = response[rows:]
+        real_pair = jnp.logical_and(row_index == 0, group == 0)
+
+        def times(first_real, first_imag, second_real, second_imag, sign):
+            both = first_imag * second_imag
+            real = first_real * second_real - jnp.where(real_pair, 0.0, sign * both)
+            imag = jnp.where(real_pair, both, first_imag * second_real + sign * first_real * second_imag)
+            return real, imag
+
+        grad_real, grad_imag = times(adjoint_real, adjoint_imag, signal_real, signal_imag, -1.0)
+        send_grad[group, :rows] = grad_real.astype(jnp.bfloat16)
+        send_grad[group, rows:] = grad_imag.astype(jnp.bfloat16)
+
+        @pl.when(group != me)
+        def _():
+            remote(2, send_grad, got_grad, me, group).start()
+
+        conv_real, conv_imag = times(signal_real, signal_imag, filter_real, filter_imag, 1.0)
+        back_real, back_imag = times(adjoint_real, adjoint_imag, filter_real, filter_imag, -1.0)
+        product = jnp.concatenate(
+            [
+                jnp.concatenate([conv_real, back_real], axis=1),
+                jnp.concatenate([conv_imag, back_imag], axis=1),
+            ],
+            axis=0,
+        ).astype(jnp.bfloat16)
+        result = dot(back_ref[group, 0], product) + dot(back_ref[group, 1], product)
+        turned[pl.ds(2 * group, 2)] = result.astype(jnp.bfloat16).reshape(2, rows, 2 * width)
+        return 0
+
+    lax.fori_loop(0, devices, one_group, 0)
+    own_grad = pltpu.make_async_copy(send_grad.at[me], got_grad.at[me], local_sems.at[0])
+    own_grad.start()
+
+    def unmix(part, _):
+        span = pl.ds(pl.multiple_of(part * SUB, SUB), SUB)
+        columns = turned[:, span, :].reshape(2 * devices * SUB, 2 * width)
+        result = dot(unmix_ref[0], columns) + dot(unmix_ref[1], columns)
+        result = result.astype(jnp.bfloat16).reshape(devices, SUB, 2 * width)
+        send_series[:, 0, span, :] = result[:, :, :width]
+        send_series[:, 1, span, :] = result[:, :, width:]
+        return 0
+
+    lax.fori_loop(0, rows // SUB, unmix, 0)
+    start_all(3, send_series, got_series)
+    own_series = pltpu.make_async_copy(send_series.at[me], got_series.at[me], local_sems.at[1])
+    own_series.start()
+    own_grad.wait()
+    own_series.wait()
+    wait_received(2, send_grad, got_grad)
+    wait_received(3, send_series, got_series)
+    for kind, source, target in (
+        (0, send_signal, got_signal),
+        (1, send_filter, got_filter),
+        (2, send_grad, got_grad),
+        (3, send_series, got_series),
+    ):
+        wait_sent(kind, source, target)
+
+
+def finish_kernel(
+    blocks,
+    width,
+    query_ref,
+    key_ref,
+    value_ref,
+    grad_ref,
+    gate_ref,
+    spread_ref,
+    half_ref,
+    series_ref,
+    mixer_out,
+    queries_out,
+    keys_out,
+    values_out,
+    spectrum_out,
+):
+    gating = gate_ref[...]
+    for block in range(blocks):
+        span = slice(block * width, (block + 1) * width)
+        conv = series_ref[block, 0].astype(jnp.float32)
+        back = series_ref[block, 1].astype(jnp.float32) * gating
+        mixer_out[:, span] = (query_ref[:, span].astype(jnp.float32) * conv).astype(jnp.bfloat16)
+        queries_out[:, span] = (grad_ref[:, span].astype(jnp.float32) * conv).astype(jnp.bfloat16)
+        keys_out[:, span] = (back * value_ref[:, span].astype(jnp.float32)).astype(jnp.bfloat16)
+        values_out[:, span] = (back * key_ref[:, span].astype(jnp.float32)).astype(jnp.bfloat16)
+        spectrum_out[:, span] = dot(spread_ref[...], half_ref[block])
+
+
+def wide_shards(query_series, key_series, value_series, grad_out, gate_mask, filter_spectrum):
+    devices = lax.axis_size("ctx")
+    rows, channels = query_series.shape
+    width = channels // devices
+    gating = gate_mask.astype(jnp.float32)[:, None]
+    mix_table, unmix_table = device_tables(devices)
+    forward_table, back_table = row_tables(devices, rows)
+    folds, spreads = fold_tables(rows)
+    first = lax.axis_index("ctx") == 0
+    fold = jnp.where(first, folds[0], folds[1])
+    spread = jnp.where(first, spreads[0], spreads[1])
+    half = jnp.bfloat16
+    vmem = pl.BlockSpec(memory_space=pltpu.VMEM)
+    anywhere = pl.BlockSpec(memory_space=pl.ANY)
+    spectrum_block = (devices, 2 * rows, width)
+    series_block = (devices, 2, rows, width)
+    got_grad, got_series = pl.pallas_call(
+        functools.partial(exchange_kernel, devices, rows, width),
+        out_shape=(
+            jax.ShapeDtypeStruct(spectrum_block, half),
+            jax.ShapeDtypeStruct(series_block, half),
+        ),
+        in_specs=[vmem] * 11,
+        out_specs=(anywhere, anywhere),
+        scratch_shapes=[
+            pltpu.VMEM(series_block, half),
+            pltpu.VMEM(series_block, half),
+            pltpu.VMEM(spectrum_block, half),
+            pltpu.VMEM(spectrum_block, half),
+            pltpu.VMEM((2 * devices, rows, 2 * width), half),
+            pltpu.VMEM((2 * devices, rows, 2 * width), half),
+            pltpu.VMEM(spectrum_block, half),
+            pltpu.VMEM(series_block, half),
+            pltpu.SemaphoreType.DMA((4, devices)),
+            pltpu.SemaphoreType.DMA((4, devices)),
+            pltpu.SemaphoreType.DMA((2,)),
+        ],
+        compiler_params=pltpu.CompilerParams(
+            collective_id=0, has_side_effects=True, vmem_limit_bytes=48 * 1024 * 1024
+        ),
+        name="exchange",
+    )(
+        query_series,
+        key_series,
+        value_series,
+        grad_out,
+        gating,
+        filter_spectrum.reshape(4 * rows, channels),
+        fold,
+        jnp.asarray(mix_table),
+        jnp.asarray(unmix_table),
+        jnp.asarray(forward_table),
+        jnp.asarray(back_table),
+    )
+    blocks = 2
+    columns = pl.BlockSpec((rows, blocks * width), lambda step: (0, step))
+    mixer_out, queries, keys, values, spectrum = pl.pallas_call(
+        functools.partial(finish_kernel, blocks, width),
+        grid=(devices // blocks,),
+        out_shape=(jax.ShapeDtypeStruct((rows, channels), half),) * 4
+        + (jax.ShapeDtypeStruct((4 * rows, channels), jnp.float32),),
+        in_specs=[
+            columns,
+            columns,
+            columns,
+            columns,
+            pl.BlockSpec((rows, 1), lambda step: (0, 0)),
+            pl.BlockSpec((4 * rows, 2 * rows), lambda step: (0, 0)),
+            pl.BlockSpec((blocks, 2 * rows, width), lambda step: (step, 0, 0)),
+            pl.BlockSpec((blocks, 2, rows, width), lambda step: (step, 0, 0, 0)),
+        ],
+        out_specs=(columns,) * 4 + (pl.BlockSpec((4 * rows, blocks * width), lambda step: (0, step)),),
+        compiler_params=pltpu.CompilerParams(vmem_limit_bytes=32 * 1024 * 1024),
+        name="finish",
+    )(query_series, key_series, value_series, grad_out, gating, spread, got_grad, got_series)
+    return mixer_out, queries, keys, values, spectrum.reshape(2, 2, rows, channels)
+
+
+def shards(query_series, *others):
+    devices = lax.axis_size("ctx")
+    rows, channels = query_series.shape
+    if rows % SUB == 0 and channels % (devices * LANES) == 0:
+        return wide_shards(query_series, *others)
+    return narrow_shards(query_series, *others)
+
+
 def solution(mesh):
     placed = (
         P(("grp", "ctx"), None),

time: 519 us -> 121 us (0.23)
  the two profiles are of different devices: /device:TPU:13 before, /device:TPU:31 now
where the time goes in v1:
time: 121 us
  Pallas kernels  111 us (92%)
  local copies, waits for them, and re-layouts  6.36 us (5%)
  other arithmetic  2.64 us (2%)
    pallas_call x1, Pallas kernels, wide_shards(): pl.pallas_call(functools.partial(exchange_kernel, devices, rows, width),...  106 us
    unnamed x12, local copies, waits for them, and re-layouts  6.24 us
    pallas_call x1, Pallas kernels, wide_shards(): pl.pallas_call(functools.partial(finish_kernel, blocks, width), grid=(dev...  5.04 us

profile of v1, /device:TPU:31, one launch (start us, length us, event | category | flops | bytes accessed | tf_op | source)
XLA Modules:
  0.0 120.9 jit_solution(12935217874499868289)
XLA Ops:
  0.6 0.7 convert_bitcast_fusion
  1.3 0.1 copy.20.gate_ref
  1.4 1.0 broadcast_select_fusion.fold_ref
  2.4 1.0 broadcast_select_fusion.1.spread_ref
  3.4 0.0 copy-start
  3.4 1.0 copy-done
  4.4 0.0 copy-start.1
  4.4 1.0 copy-done.1
  5.5 0.0 copy-start.2
  5.5 1.0 copy-done.2
  6.5 0.0 copy-start.3
  6.5 1.0 copy-done.3
  7.6 0.0 copy-start.4
  7.6 1.0 copy-done.4
  8.6 0.0 copy-start.5
  8.6 1.0 copy-done.5
  9.7 106.2 %exchange.1 = (bf16[16,256,128]{2,1,0:T(8,128)(2,1)S(1)}, bf16[16,2,128,128]{3,2,1,0:T(8,128)(2,1)S(1)}) custom-call(bf16[128,2048]{1,0:T(8,128)(2,1)S(1)} %copy-done, bf16[128,2048]{1,0:T(8,128)(2,1)S(1)} %copy-done.1, bf16[128,2048]{1,0:T(8,128)(2,1)S(1)} %copy-done.2, bf16[128,2048]{1,0:T(8,128)(2,1)S(1)} %copy-done.3, f32[128,1]{1,0:T(8,128)S(1)} %copy.20.gate_ref, ...), custom_call_target="tpu_custom_call" | custom-call | tf_op jit(solution)/shard_map/exchange/pallas_call | solution.py:472
  115.9 5.0 %finish.1 = (bf16[128,2048]{1,0:T(8,128)(2,1)}, bf16[128,2048]{1,0:T(8,128)(2,1)}, bf16[128,2048]{1,0:T(8,128)(2,1)}, bf16[128,2048]{1,0:T(8,128)(2,1)}, f32[512,2048]{1,0:T(8,128)}) custom-call(bf16[128,2048]{1,0:T(8,128)(2,1)S(1)} %copy-done, bf16[128,2048]{1,0:T(8,128)(2,1)S(1)} %copy-done.1, bf16[128,2048]{1,0:T(8,128)(2,1)S(1)} %copy-done.2, ...), custom_call_target="tpu_custom_call" | custom-call | tf_op jit(solution)/shard_map/finish/pallas_call | solution.py:512
Async XLA Ops:
  3.4 1.0 copy-start
  4.4 1.0 copy-start.1
  5.5 1.0 copy-start.2
  6.5 1.0 copy-start.3
  7.6 1.0 copy-start.4
  8.6 1.0 copy-start.5

commit v2 on v1

--- a/solution.py
+++ b/solution.py
@@ -245,21 +245,32 @@
 
 def exchange_kernel(
     devices,
+    groups,
     rows,
     width,
+    gate_ref,
+    query_hbm,
+    key_hbm,
+    value_hbm,
+    grad_hbm,
+    fold_hbm,
+    filter_hbm,
+    mix_hbm,
+    table_hbm,
+    back_hbm,
+    unmix_hbm,
+    got_grad,
+    got_series,
     query_ref,
     key_ref,
     value_ref,
     grad_ref,
-    gate_ref,
+    fold_ref,
     filter_ref,
-    fold_ref,
     mix_ref,
-    unmix_ref,
     table_ref,
     back_ref,
-    got_grad,
-    got_series,
+    unmix_ref,
     send_signal,
     got_signal,
     send_filter,
@@ -273,7 +284,28 @@
     local_sems,
 ):
     me = lax.axis_index("ctx")
+    lane = lax.axis_index("grp")
     barrier = pltpu.get_barrier_semaphore()
+    own_fold = jnp.where(me == 0, 0, 1)
+    loads = [
+        pltpu.make_async_copy(source, target, local_sems.at[2 + at])
+        for at, (source, target) in enumerate(
+            (
+                (query_hbm, query_ref),
+                (key_hbm, key_ref),
+                (value_hbm, value_ref),
+                (grad_hbm, grad_ref),
+                (fold_hbm.at[own_fold], fold_ref),
+                (filter_hbm, filter_ref),
+                (mix_hbm, mix_ref),
+                (table_hbm, table_ref),
+                (back_hbm, back_ref),
+                (unmix_hbm, unmix_ref),
+            )
+        )
+    ]
+    for load in loads:
+        load.start()
 
     def greet(step, _):
         pl.semaphore_signal(
@@ -285,6 +317,13 @@
         return 0
 
     lax.fori_loop(1, devices, greet, 0)
+    for step in range(1, groups):
+        pl.semaphore_signal(
+            barrier,
+            inc=1,
+            device_id={"grp": lax.rem(lane + step, groups)},
+            device_id_type=pl.DeviceIdType.MESH,
+        )
 
     def remote(kind, source, target, step_from, to):
         return pltpu.make_async_remote_copy(
@@ -296,6 +335,16 @@
             device_id_type=pl.DeviceIdType.MESH,
         )
 
+    def relay(step, group):
+        return pltpu.make_async_remote_copy(
+            src_ref=got_filter.at[group],
+            dst_ref=got_filter.at[group],
+            send_sem=send_sems.at[3 + step, group],
+            recv_sem=recv_sems.at[1, group],
+            device_id={"grp": lax.rem(lane + step, groups)},
+            device_id_type=pl.DeviceIdType.MESH,
+        )
+
     def start_all(kind, source, target):
         def body(step, _):
             remote(kind, source, target, me, lax.rem(me + step, devices)).start()
@@ -318,6 +367,8 @@
 
         lax.fori_loop(1, devices, body, 0)
 
+    for load in loads[:4]:
+        load.wait()
     gating = gate_ref[...]
     for to in range(devices):
         span = slice(to * width, (to + 1) * width)
@@ -325,20 +376,28 @@
         back = query_ref[:, span].astype(jnp.float32) * grad_ref[:, span].astype(jnp.float32)
         send_signal[to, 0] = gated.astype(jnp.bfloat16)
         send_signal[to, 1] = back.astype(jnp.bfloat16)
-    pl.semaphore_wait(barrier, devices - 1)
+    pl.semaphore_wait(barrier, devices + groups - 2)
     start_all(0, send_signal, got_signal)
     got_signal[me] = send_signal[me]
 
-    for to in range(devices):
-        span = slice(to * width, (to + 1) * width)
-        block = filter_ref[:, span]
-        high = block.astype(jnp.bfloat16)
-        low = (block - high.astype(jnp.float32)).astype(jnp.bfloat16)
-        folded = dot(fold_ref[...], high) + dot(fold_ref[...], low)
-        send_filter[to] = folded.astype(jnp.bfloat16)
-    start_all(1, send_filter, got_filter)
-    got_filter[me] = send_filter[me]
-
+    for load in loads[4:6]:
+        load.wait()
+    mine = lax.rem(me, groups) == lane
+
+    @pl.when(mine)
+    def _():
+        for to in range(devices):
+            span = slice(to * width, (to + 1) * width)
+            block = filter_ref[:, span]
+            high = block.astype(jnp.bfloat16)
+            low = (block - high.astype(jnp.float32)).astype(jnp.bfloat16)
+            folded = dot(fold_ref[...], high) + dot(fold_ref[...], low)
+            send_filter[to] = folded.astype(jnp.bfloat16)
+        start_all(1, send_filter, got_filter)
+        got_filter[me] = send_filter[me]
+
+    for load in loads[6:]:
+        load.wait()
     wait_received(0, send_signal, got_signal)
 
     def mix(part, _):
@@ -351,11 +410,10 @@
         return 0
 
     lax.fori_loop(0, rows // SUB, mix, 0)
-    wait_received(1, send_filter, got_filter)
 
     row_index = lax.broadcasted_iota(jnp.int32, (rows, width), 0)
 
-    def one_group(group, _):
+    def one_group(group):
         source = mixed[pl.ds(2 * group, 2)].reshape(2 * rows, 2 * width)
         spectra = dot(table_ref[group, 0], source) + dot(table_ref[group, 1], source)
         signal_real = spectra[:rows, :width]
@@ -392,9 +450,31 @@
         ).astype(jnp.bfloat16)
         result = dot(back_ref[group, 0], product) + dot(back_ref[group, 1], product)
         turned[pl.ds(2 * group, 2)] = result.astype(jnp.bfloat16).reshape(2, rows, 2 * width)
-        return 0
-
-    lax.fori_loop(0, devices, one_group, 0)
+
+    def in_turn(shift):
+        share = lax.rem(lane + shift, groups)
+
+        def body(turn, _):
+            place = lax.rem(me // groups + devices // groups - turn, devices // groups)
+            group = place * groups + share
+
+            if shift == 0:
+
+                @pl.when(group != me)
+                def _():
+                    remote(1, send_filter, got_filter, group, group).wait_recv()
+
+                for step in range(1, groups):
+                    relay(step, group).start()
+            else:
+                relay(shift, group).wait_recv()
+            one_group(group)
+            return 0
+
+        return body
+
+    for shift in range(groups):
+        lax.fori_loop(0, devices // groups, in_turn(shift), 0)
     own_grad = pltpu.make_async_copy(send_grad.at[me], got_grad.at[me], local_sems.at[0])
     own_grad.start()
 
@@ -415,13 +495,20 @@
     own_series.wait()
     wait_received(2, send_grad, got_grad)
     wait_received(3, send_series, got_series)
-    for kind, source, target in (
-        (0, send_signal, got_signal),
-        (1, send_filter, got_filter),
-        (2, send_grad, got_grad),
-        (3, send_series, got_series),
-    ):
-        wait_sent(kind, source, target)
+    wait_sent(0, send_signal, got_signal)
+
+    @pl.when(mine)
+    def _():
+        wait_sent(1, send_filter, got_filter)
+
+    def relays_sent(turn, _):
+        for step in range(1, groups):
+            relay(step, turn * groups + lane).wait_send()
+        return 0
+
+    lax.fori_loop(0, devices // groups, relays_sent, 0)
+    wait_sent(2, send_grad, got_grad)
+    wait_sent(3, send_series, got_series)
 
 
 def finish_kernel(
@@ -442,6 +529,7 @@
     spectrum_out,
 ):
     gating = gate_ref[...]
+    own_spread = jnp.where(lax.axis_index("ctx") == 0, 0, 1)
     for block in range(blocks):
         span = slice(block * width, (block + 1) * width)
         conv = series_ref[block, 0].astype(jnp.float32)
@@ -450,7 +538,7 @@
         queries_out[:, span] = (grad_ref[:, span].astype(jnp.float32) * conv).astype(jnp.bfloat16)
         keys_out[:, span] = (back * value_ref[:, span].astype(jnp.float32)).astype(jnp.bfloat16)
         values_out[:, span] = (back * key_ref[:, span].astype(jnp.float32)).astype(jnp.bfloat16)
-        spectrum_out[:, span] = dot(spread_ref[...], half_ref[block])
+        spectrum_out[:, span] = dot(spread_ref[own_spread], half_ref[block])
 
 
 def wide_shards(query_series, key_series, value_series, grad_out, gate_mask, filter_spectrum):
@@ -461,23 +549,28 @@
     mix_table, unmix_table = device_tables(devices)
     forward_table, back_table = row_tables(devices, rows)
     folds, spreads = fold_tables(rows)
-    first = lax.axis_index("ctx") == 0
-    fold = jnp.where(first, folds[0], folds[1])
-    spread = jnp.where(first, spreads[0], spreads[1])
+    groups = lax.axis_size("grp")
     half = jnp.bfloat16
     vmem = pl.BlockSpec(memory_space=pltpu.VMEM)
     anywhere = pl.BlockSpec(memory_space=pl.ANY)
     spectrum_block = (devices, 2 * rows, width)
     series_block = (devices, 2, rows, width)
     got_grad, got_series = pl.pallas_call(
-        functools.partial(exchange_kernel, devices, rows, width),
+        functools.partial(exchange_kernel, devices, groups, rows, width),
         out_shape=(
             jax.ShapeDtypeStruct(spectrum_block, half),
             jax.ShapeDtypeStruct(series_block, half),
         ),
-        in_specs=[vmem] * 11,
+        in_specs=[vmem] + [anywhere] * 10,
         out_specs=(anywhere, anywhere),
-        scratch_shapes=[
+        scratch_shapes=[pltpu.VMEM((rows, channels), half)] * 4
+        + [
+            pltpu.VMEM((2 * rows, 4 * rows), half),
+            pltpu.VMEM((4 * rows, channels), jnp.float32),
+            pltpu.VMEM(mix_table.shape, half),
+            pltpu.VMEM(forward_table.shape, half),
+            pltpu.VMEM(back_table.shape, half),
+            pltpu.VMEM(unmix_table.shape, half),
             pltpu.VMEM(series_block, half),
             pltpu.VMEM(series_block, half),
             pltpu.VMEM(spectrum_block, half),
@@ -486,26 +579,26 @@
             pltpu.VMEM((2 * devices, rows, 2 * width), half),
             pltpu.VMEM(spectrum_block, half),
             pltpu.VMEM(series_block, half),
+            pltpu.SemaphoreType.DMA((3 + groups, devices)),
             pltpu.SemaphoreType.DMA((4, devices)),
-            pltpu.SemaphoreType.DMA((4, devices)),
-            pltpu.SemaphoreType.DMA((2,)),
+            pltpu.SemaphoreType.DMA((12,)),
         ],
         compiler_params=pltpu.CompilerParams(
-            collective_id=0, has_side_effects=True, vmem_limit_bytes=48 * 1024 * 1024
+            collective_id=0, has_side_effects=True, vmem_limit_bytes=60 * 1024 * 1024
         ),
         name="exchange",
     )(
+        gating,
         query_series,
         key_series,
         value_series,
         grad_out,
-        gating,
+        jnp.asarray(folds),
         filter_spectrum.reshape(4 * rows, channels),
-        fold,
         jnp.asarray(mix_table),
-        jnp.asarray(unmix_table),
         jnp.asarray(forward_table),
         jnp.asarray(back_table),
+        jnp.asarray(unmix_table),
     )
     blocks = 2
     columns = pl.BlockSpec((rows, blocks * width), lambda step: (0, step))
@@ -520,21 +613,21 @@
             columns,
             columns,
             pl.BlockSpec((rows, 1), lambda step: (0, 0)),
-            pl.BlockSpec((4 * rows, 2 * rows), lambda step: (0, 0)),
+            pl.BlockSpec((2, 4 * rows, 2 * rows), lambda step: (0, 0, 0)),
             pl.BlockSpec((blocks, 2 * rows, width), lambda step: (step, 0, 0)),
             pl.BlockSpec((blocks, 2, rows, width), lambda step: (step, 0, 0, 0)),
         ],
         out_specs=(columns,) * 4 + (pl.BlockSpec((4 * rows, blocks * width), lambda step: (0, step)),),
-        compiler_params=pltpu.CompilerParams(vmem_limit_bytes=32 * 1024 * 1024),
+        compiler_params=pltpu.CompilerParams(vmem_limit_bytes=60 * 1024 * 1024),
         name="finish",
-    )(query_series, key_series, value_series, grad_out, gating, spread, got_grad, got_series)
+    )(query_series, key_series, value_series, grad_out, gating, jnp.asarray(spreads), got_grad, got_series)
     return mixer_out, queries, keys, values, spectrum.reshape(2, 2, rows, channels)
 
 
 def shards(query_series, *others):
     devices = lax.axis_size("ctx")
     rows, channels = query_series.shape
-    if rows % SUB == 0 and channels % (devices * LANES) == 0:
+    if rows % SUB == 0 and channels % (devices * LANES) == 0 and devices % lax.axis_size("grp") == 0:
         return wide_shards(query_series, *others)
     return narrow_shards(query_series, *others)
 

time: 121 us -> 105 us (0.87)
  the two profiles are of different devices: /device:TPU:31 before, /device:TPU:15 now
where the time goes in v2:
time: 105 us
  Pallas kernels  103 us (98%)
    pallas_call x1, Pallas kernels, wide_shards(): pl.pallas_call(functools.partial(exchange_kernel, devices, groups, rows,...  94.2 us
    pallas_call x1, Pallas kernels, wide_shards(): pl.pallas_call(functools.partial(finish_kernel, blocks, width), grid=(dev...  8.57 us

profile of v2, /device:TPU:15, one launch (start us, length us, event | category | flops | bytes accessed | tf_op | source)
XLA Modules:
  0.0 104.8 jit_solution(8581752939473742489)
XLA Ops:
  0.6 0.7 convert_bitcast_fusion
  1.3 0.7 copy.18.gate_ref
  2.0 94.2 %exchange.1 = (bf16[16,256,128]{2,1,0:T(8,128)(2,1)}, bf16[16,2,128,128]{3,2,1,0:T(8,128)(2,1)}) custom-call(f32[128,1]{1,0:T(8,128)} %copy.18.gate_ref, bf16[128,2048]{1,0:T(8,128)(2,1)} %query_ref.1, bf16[128,2048]{1,0:T(8,128)(2,1)} %key_ref.1, bf16[128,2048]{1,0:T(8,128)(2,1)} %value_ref.1, bf16[128,2048]{1,0:T(8,128)(2,1)} %grad_ref.1, ...), custom_call_target="tpu_custom_call" | custom-call | tf_op jit(solution)/shard_map/exchange/pallas_call | solution.py:558
  96.2 8.6 %finish.1 = (bf16[128,2048]{1,0:T(8,128)(2,1)}, bf16[128,2048]{1,0:T(8,128)(2,1)}, bf16[128,2048]{1,0:T(8,128)(2,1)}, bf16[128,2048]{1,0:T(8,128)(2,1)}, f32[512,2048]{1,0:T(8,128)}) custom-call(bf16[128,2048]{1,0:T(8,128)(2,1)} %query_ref.1, bf16[128,2048]{1,0:T(8,128)(2,1)} %key_ref.1, bf16[128,2048]{1,0:T(8,128)(2,1)} %value_ref.1, ...), custom_call_target="tpu_custom_call" | custom-call | tf_op jit(solution)/shard_map/finish/pallas_call | solution.py:605

commit v3 on v2

--- a/solution.py
+++ b/solution.py
@@ -241,6 +241,14 @@
 
 def dot(left, right):
     return jnp.dot(left, right, preferred_element_type=jnp.float32)
+
+
+def gate_column(mask):
+    rows = mask.shape[1]
+    across = lax.broadcasted_iota(jnp.int32, (rows, rows), 1)
+    down = lax.broadcasted_iota(jnp.int32, (rows, rows), 0)
+    spots = jnp.where(across == down, mask.astype(jnp.float32), 0.0)
+    return jnp.sum(spots, axis=1, keepdims=True)
 
 
 def exchange_kernel(
@@ -325,6 +333,15 @@
             device_id_type=pl.DeviceIdType.MESH,
         )
 
+    near = devices // 2
+    side = me // near
+    spot = lax.rem(me, near)
+
+    def partner_at(step, direction):
+        step = step + step // near
+        half_at = lax.rem(side + 1 + step // near, 2)
+        return half_at * near + lax.rem(spot + near + direction * lax.rem(step, near), near)
+
     def remote(kind, source, target, step_from, to):
         return pltpu.make_async_remote_copy(
             src_ref=source.at[to],
@@ -347,29 +364,29 @@
 
     def start_all(kind, source, target):
         def body(step, _):
-            remote(kind, source, target, me, lax.rem(me + step, devices)).start()
+            remote(kind, source, target, me, partner_at(step, 1)).start()
             return 0
 
-        lax.fori_loop(1, devices, body, 0)
-
-    def wait_received(kind, source, target, first=1):
+        lax.fori_loop(0, devices - 1, body, 0)
+
+    def wait_received(kind, source, target):
         def body(step, _):
-            other = lax.rem(me + devices - step, devices)
+            other = partner_at(step, -1)
             remote(kind, source, target, other, other).wait_recv()
             return 0
 
-        lax.fori_loop(first, devices, body, 0)
+        lax.fori_loop(0, devices - 1, body, 0)
 
     def wait_sent(kind, source, target):
         def body(step, _):
-            remote(kind, source, target, me, lax.rem(me + step, devices)).wait_send()
+            remote(kind, source, target, me, partner_at(step, 1)).wait_send()
             return 0
 
-        lax.fori_loop(1, devices, body, 0)
+        lax.fori_loop(0, devices - 1, body, 0)
 
     for load in loads[:4]:
         load.wait()
-    gating = gate_ref[...]
+    gating = gate_column(gate_ref[...])
     for to in range(devices):
         span = slice(to * width, (to + 1) * width)
         gated = gating * key_ref[:, span].astype(jnp.float32) * value_ref[:, span].astype(jnp.float32)
@@ -451,12 +468,15 @@
         result = dot(back_ref[group, 0], product) + dot(back_ref[group, 1], product)
         turned[pl.ds(2 * group, 2)] = result.astype(jnp.bfloat16).reshape(2, rows, 2 * width)
 
+    turns = near // groups
+
     def in_turn(shift):
         share = lax.rem(lane + shift, groups)
 
         def body(turn, _):
-            place = lax.rem(me // groups + devices // groups - turn, devices // groups)
-            group = place * groups + share
+            half_at = lax.rem(side + 1 + turn // turns, 2)
+            place = lax.rem(spot // groups + turns - lax.rem(turn, turns), turns)
+            group = half_at * near + place * groups + share
 
             if shift == 0:
 
@@ -528,7 +548,7 @@
     values_out,
     spectrum_out,
 ):
-    gating = gate_ref[...]
+    gating = gate_column(gate_ref[...])
     own_spread = jnp.where(lax.axis_index("ctx") == 0, 0, 1)
     for block in range(blocks):
         span = slice(block * width, (block + 1) * width)
@@ -545,7 +565,7 @@
     devices = lax.axis_size("ctx")
     rows, channels = query_series.shape
     width = channels // devices
-    gating = gate_mask.astype(jnp.float32)[:, None]
+    gating = gate_mask[None, :]
     mix_table, unmix_table = device_tables(devices)
     forward_table, back_table = row_tables(devices, rows)
     folds, spreads = fold_tables(rows)
@@ -612,13 +632,13 @@
             columns,
             columns,
             columns,
-            pl.BlockSpec((rows, 1), lambda step: (0, 0)),
+            pl.BlockSpec((1, rows), lambda step: (0, 0)),
             pl.BlockSpec((2, 4 * rows, 2 * rows), lambda step: (0, 0, 0)),
             pl.BlockSpec((blocks, 2 * rows, width), lambda step: (step, 0, 0)),
             pl.BlockSpec((blocks, 2, rows, width), lambda step: (step, 0, 0, 0)),
         ],
         out_specs=(columns,) * 4 + (pl.BlockSpec((4 * rows, blocks * width), lambda step: (0, step)),),
-        compiler_params=pltpu.CompilerParams(vmem_limit_bytes=60 * 1024 * 1024),
+        compiler_params=pltpu.CompilerParams(vmem_limit_bytes=32 * 1024 * 1024),
         name="finish",
     )(query_series, key_series, value_series, grad_out, gating, jnp.asarray(spreads), got_grad, got_series)
     return mixer_out, queries, keys, values, spectrum.reshape(2, 2, rows, channels)
@@ -627,7 +647,7 @@
 def shards(query_series, *others):
     devices = lax.axis_size("ctx")
     rows, channels = query_series.shape
-    if rows % SUB == 0 and channels % (devices * LANES) == 0 and devices % lax.axis_size("grp") == 0:
+    if rows % SUB == 0 and channels % (devices * LANES) == 0 and devices % (2 * lax.axis_size("grp")) == 0:
         return wide_shards(query_series, *others)
     return narrow_shards(query_series, *others)
 

time: 105 us -> 98.3 us (0.936)
  the two profiles are of different devices: /device:TPU:15 before, /device:TPU:0 now
where the time goes in v3:
time: 98.3 us; the launch traced here: 98.1 us
  Pallas kernels  94.9 us (97%)
  local copies, waits for them, and re-layouts  2.47 us (3%)
    pallas_call x1, Pallas kernels, wide_shards(): pl.pallas_call(functools.partial(exchange_kernel, devices, groups, rows,...  89.8 us
    pallas_call x1, Pallas kernels, wide_shards(): pl.pallas_call(functools.partial(finish_kernel, blocks, width), grid=(dev...  5.08 us
    unnamed x16, local copies, waits for them, and re-layouts  2.47 us

profile of v3, /device:TPU:0, one launch (start us, length us, event | category | flops | bytes accessed | tf_op | source)
XLA Modules:
  0.0 98.1 jit_solution(14642258460001819621)
XLA Ops:
  0.6 0.0 copy-start
  0.6 0.0 copy-start.1
  0.7 0.0 copy-start.2
  0.7 0.0 copy-start.3
  0.7 0.0 copy-start.6
  0.7 0.0 copy-start.7
  0.7 89.8 %exchange.1 = (bf16[16,256,128]{2,1,0:T(8,128)(2,1)}, bf16[16,2,128,128]{3,2,1,0:T(8,128)(2,1)}) custom-call(s32[1,128]{1,0:T(1,128)} %bitcast.3, bf16[128,2048]{1,0:T(8,128)(2,1)} %query_ref.1, bf16[128,2048]{1,0:T(8,128)(2,1)} %key_ref.1, bf16[128,2048]{1,0:T(8,128)(2,1)} %value_ref.1, bf16[128,2048]{1,0:T(8,128)(2,1)} %grad_ref.1, ...), custom_call_target="tpu_custom_call" | custom-call | tf_op jit(solution)/shard_map/exchange/pallas_call | solution.py:578
  90.5 0.0 copy-done
  90.5 0.0 copy-done.1
  90.5 0.0 copy-done.2
  90.5 0.0 copy-done.3
  90.5 0.0 copy-done.6
  90.5 0.0 copy-done.7
  90.6 0.0 copy-start.4
  90.6 1.2 %copy-done.4 = bf16[16,256,128]{2,1,0:T(8,128)(2,1)S(1)} copy-done((bf16[16,256,128]{2,1,0:T(8,128)(2,1)S(1)}, bf16[16,256,128]{2,1,0:T(8,128)(2,1)}, u32[]{:S(2)}) %copy-start.4) | copy-done | bytes 1048600
  91.8 0.0 copy-start.5
  91.8 1.2 %copy-done.5 = bf16[16,2,128,128]{3,2,1,0:T(8,128)(2,1)S(1)} copy-done((bf16[16,2,128,128]{3,2,1,0:T(8,128)(2,1)S(1)}, bf16[16,2,128,128]{3,2,1,0:T(8,128)(2,1)}, u32[]{:S(2)}) %copy-start.5) | copy-done | bytes 1048600
  93.0 5.1 %finish.1 = (bf16[128,2048]{1,0:T(8,128)(2,1)}, bf16[128,2048]{1,0:T(8,128)(2,1)}, bf16[128,2048]{1,0:T(8,128)(2,1)}, bf16[128,2048]{1,0:T(8,128)(2,1)}, f32[512,2048]{1,0:T(8,128)}) custom-call(bf16[128,2048]{1,0:T(8,128)(2,1)S(1)} %copy-done, bf16[128,2048]{1,0:T(8,128)(2,1)S(1)} %copy-done.1, bf16[128,2048]{1,0:T(8,128)(2,1)S(1)} %copy-done.2, ...), custom_call_target="tpu_custom_call" | custom-call | tf_op jit(solution)/shard_map/finish/pallas_call | solution.py:625
Async XLA Ops:
  0.6 89.9 %copy-start = (bf16[128,2048]{1,0:T(8,128)(2,1)S(1)}, bf16[128,2048]{1,0:T(8,128)(2,1)}, u32[]{:S(2)}) copy-start(bf16[128,2048]{1,0:T(8,128)(2,1)} %query_ref.1) | copy-start | bytes 1572868
  0.6 89.9 %copy-start.1 = (bf16[128,2048]{1,0:T(8,128)(2,1)S(1)}, bf16[128,2048]{1,0:T(8,128)(2,1)}, u32[]{:S(2)}) copy-start(bf16[128,2048]{1,0:T(8,128)(2,1)} %key_ref.1) | copy-start | bytes 1572868
  0.7 89.9 %copy-start.2 = (bf16[128,2048]{1,0:T(8,128)(2,1)S(1)}, bf16[128,2048]{1,0:T(8,128)(2,1)}, u32[]{:S(2)}) copy-start(bf16[128,2048]{1,0:T(8,128)(2,1)} %value_ref.1) | copy-start | bytes 1572868
  0.7 89.9 %copy-start.3 = (bf16[128,2048]{1,0:T(8,128)(2,1)S(1)}, bf16[128,2048]{1,0:T(8,128)(2,1)}, u32[]{:S(2)}) copy-start(bf16[128,2048]{1,0:T(8,128)(2,1)} %grad_ref.1) | copy-start | bytes 1572868
  0.7 89.9 %copy-start.6 = (bf16[2,512,256]{2,1,0:T(8,128)(2,1)S(1)}, bf16[2,512,256]{2,1,0:T(8,128)(2,1)}, u32[]{:S(2)}) copy-start(bf16[2,512,256]{2,1,0:T(8,128)(2,1)} %constant.17.clone.spread_ref) | copy-start | bytes 1572868
  0.7 89.9 %copy-start.7 = (s32[128]{0:T(128)S(1)}, s32[128]{0:T(128)}, u32[]{:S(2)}) copy-start(s32[128]{0:T(128)} %param.16) | copy-start | bytes 1540
  90.6 1.2 %copy-start.4 = (bf16[16,256,128]{2,1,0:T(8,128)(2,1)S(1)}, bf16[16,256,128]{2,1,0:T(8,128)(2,1)}, u32[]{:S(2)}) copy-start(bf16[16,256,128]{2,1,0:T(8,128)(2,1)} %get-tuple-element.12.half_ref) | copy-start | bytes 3145732
  91.8 1.2 %copy-start.5 = (bf16[16,2,128,128]{3,2,1,0:T(8,128)(2,1)S(1)}, bf16[16,2,128,128]{3,2,1,0:T(8,128)(2,1)}, u32[]{:S(2)}) copy-start(bf16[16,2,128,128]{3,2,1,0:T(8,128)(2,1)} %get-tuple-element.13.series_ref) | copy-start | bytes 3145732

commit v4 on v3

--- a/solution.py
+++ b/solution.py
@@ -267,8 +267,9 @@
     table_hbm,
     back_hbm,
     unmix_hbm,
-    got_grad,
+    spread_hbm,
     got_series,
+    spectrum_hbm,
     query_ref,
     key_ref,
     value_ref,
@@ -279,6 +280,8 @@
     table_ref,
     back_ref,
     unmix_ref,
+    spread_ref,
+    got_grad,
     send_signal,
     got_signal,
     send_filter,
@@ -309,6 +312,7 @@
                 (table_hbm, table_ref),
                 (back_hbm, back_ref),
                 (unmix_hbm, unmix_ref),
+                (spread_hbm.at[own_fold], spread_ref),
             )
         )
     ]
@@ -387,15 +391,26 @@
     for load in loads[:4]:
         load.wait()
     gating = gate_column(gate_ref[...])
-    for to in range(devices):
-        span = slice(to * width, (to + 1) * width)
+
+    def columns_of(block):
+        return pl.ds(pl.multiple_of(block * width, width), width)
+
+    def make_signal(to):
+        span = columns_of(to)
         gated = gating * key_ref[:, span].astype(jnp.float32) * value_ref[:, span].astype(jnp.float32)
         back = query_ref[:, span].astype(jnp.float32) * grad_ref[:, span].astype(jnp.float32)
-        send_signal[to, 0] = gated.astype(jnp.bfloat16)
-        send_signal[to, 1] = back.astype(jnp.bfloat16)
+        return gated.astype(jnp.bfloat16), back.astype(jnp.bfloat16)
+
     pl.semaphore_wait(barrier, devices + groups - 2)
-    start_all(0, send_signal, got_signal)
-    got_signal[me] = send_signal[me]
+
+    def ship_signal(step, _):
+        to = partner_at(step, 1)
+        send_signal[to, 0], send_signal[to, 1] = make_signal(to)
+        remote(0, send_signal, got_signal, me, to).start()
+        return 0
+
+    lax.fori_loop(0, devices - 1, ship_signal, 0)
+    got_signal[me, 0], got_signal[me, 1] = make_signal(me)
 
     for load in loads[4:6]:
         load.wait()
@@ -495,8 +510,7 @@
 
     for shift in range(groups):
         lax.fori_loop(0, devices // groups, in_turn(shift), 0)
-    own_grad = pltpu.make_async_copy(send_grad.at[me], got_grad.at[me], local_sems.at[0])
-    own_grad.start()
+    got_grad[me] = send_grad[me]
 
     def unmix(part, _):
         span = pl.ds(pl.multiple_of(part * SUB, SUB), SUB)
@@ -511,9 +525,21 @@
     start_all(3, send_series, got_series)
     own_series = pltpu.make_async_copy(send_series.at[me], got_series.at[me], local_sems.at[1])
     own_series.start()
-    own_grad.wait()
+
+    def spread_block(other):
+        filter_ref[:, columns_of(other)] = dot(spread_ref[...], got_grad[other])
+
+    def spread_next(step, _):
+        other = partner_at(step, -1)
+        remote(2, send_grad, got_grad, other, other).wait_recv()
+        spread_block(other)
+        return 0
+
+    spread_block(me)
+    lax.fori_loop(0, devices - 1, spread_next, 0)
+    spectrum_copy = pltpu.make_async_copy(filter_ref, spectrum_hbm, local_sems.at[0])
+    spectrum_copy.start()
     own_series.wait()
-    wait_received(2, send_grad, got_grad)
     wait_received(3, send_series, got_series)
     wait_sent(0, send_signal, got_signal)
 
@@ -529,6 +555,7 @@
     lax.fori_loop(0, devices // groups, relays_sent, 0)
     wait_sent(2, send_grad, got_grad)
     wait_sent(3, send_series, got_series)
+    spectrum_copy.wait()
 
 
 def finish_kernel(
@@ -539,17 +566,13 @@
     value_ref,
     grad_ref,
     gate_ref,
-    spread_ref,
-    half_ref,
     series_ref,
     mixer_out,
     queries_out,
     keys_out,
     values_out,
-    spectrum_out,
 ):
     gating = gate_column(gate_ref[...])
-    own_spread = jnp.where(lax.axis_index("ctx") == 0, 0, 1)
     for block in range(blocks):
         span = slice(block * width, (block + 1) * width)
         conv = series_ref[block, 0].astype(jnp.float32)
@@ -558,7 +581,6 @@
         queries_out[:, span] = (grad_ref[:, span].astype(jnp.float32) * conv).astype(jnp.bfloat16)
         keys_out[:, span] = (back * value_ref[:, span].astype(jnp.float32)).astype(jnp.bfloat16)
         values_out[:, span] = (back * key_ref[:, span].astype(jnp.float32)).astype(jnp.bfloat16)
-        spectrum_out[:, span] = dot(spread_ref[own_spread], half_ref[block])
 
 
 def wide_shards(query_series, key_series, value_series, grad_out, gate_mask, filter_spectrum):
@@ -575,13 +597,13 @@
     anywhere = pl.BlockSpec(memory_space=pl.ANY)
     spectrum_block = (devices, 2 * rows, width)
     series_block = (devices, 2, rows, width)
-    got_grad, got_series = pl.pallas_call(
+    got_series, spectrum = pl.pallas_call(
         functools.partial(exchange_kernel, devices, groups, rows, width),
         out_shape=(
-            jax.ShapeDtypeStruct(spectrum_block, half),
             jax.ShapeDtypeStruct(series_block, half),
+            jax.ShapeDtypeStruct((4 * rows, channels), jnp.float32),
         ),
-        in_specs=[vmem] + [anywhere] * 10,
+        in_specs=[vmem] + [anywhere] * 11,
         out_specs=(anywhere, anywhere),
         scratch_shapes=[pltpu.VMEM((rows, channels), half)] * 4
         + [
@@ -591,6 +613,8 @@
             pltpu.VMEM(forward_table.shape, half),
             pltpu.VMEM(back_table.shape, half),
             pltpu.VMEM(unmix_table.shape, half),
+            pltpu.VMEM((4 * rows, 2 * rows), half),
+            pltpu.VMEM(spectrum_block, half),
             pltpu.VMEM(series_block, half),
             pltpu.VMEM(series_block, half),
             pltpu.VMEM(spectrum_block, half),
@@ -601,7 +625,7 @@
             pltpu.VMEM(series_block, half),
             pltpu.SemaphoreType.DMA((3 + groups, devices)),
             pltpu.SemaphoreType.DMA((4, devices)),
-            pltpu.SemaphoreType.DMA((12,)),
+            pltpu.SemaphoreType.DMA((13,)),
         ],
         compiler_params=pltpu.CompilerParams(
             collective_id=0, has_side_effects=True, vmem_limit_bytes=60 * 1024 * 1024
@@ -619,28 +643,26 @@
         jnp.asarray(forward_table),
         jnp.asarray(back_table),
         jnp.asarray(unmix_table),
-    )
-    blocks = 2
+        jnp.asarray(spreads),
+    )
+    blocks = math.gcd(devices, 4)
     columns = pl.BlockSpec((rows, blocks * width), lambda step: (0, step))
-    mixer_out, queries, keys, values, spectrum = pl.pallas_call(
+    mixer_out, queries, keys, values = pl.pallas_call(
         functools.partial(finish_kernel, blocks, width),
         grid=(devices // blocks,),
-        out_shape=(jax.ShapeDtypeStruct((rows, channels), half),) * 4
-        + (jax.ShapeDtypeStruct((4 * rows, channels), jnp.float32),),
+        out_shape=(jax.ShapeDtypeStruct((rows, channels), half),) * 4,
         in_specs=[
             columns,
             columns,
             columns,
             columns,
             pl.BlockSpec((1, rows), lambda step: (0, 0)),
-            pl.BlockSpec((2, 4 * rows, 2 * rows), lambda step: (0, 0, 0)),
-            pl.BlockSpec((blocks, 2 * rows, width), lambda step: (step, 0, 0)),
             pl.BlockSpec((blocks, 2, rows, width), lambda step: (step, 0, 0, 0)),
         ],
-        out_specs=(columns,) * 4 + (pl.BlockSpec((4 * rows, blocks * width), lambda step: (0, step)),),
+        out_specs=(columns,) * 4,
         compiler_params=pltpu.CompilerParams(vmem_limit_bytes=32 * 1024 * 1024),
         name="finish",
-    )(query_series, key_series, value_series, grad_out, gating, jnp.asarray(spreads), got_grad, got_series)
+    )(query_series, key_series, value_series, grad_out, gating, got_series)
     return mixer_out, queries, keys, values, spectrum.reshape(2, 2, rows, channels)
 
 

time: 98.3 us -> 99.8 us (1.015)
  local copies, waits for them, and re-layouts: 2.47 us -> 5.94 us
  Pallas kernels: 94.9 us -> 92.9 us
    unnamed x16 -> x13, local copies, waits for them, and re-layouts: 2.47 us -> 5.94 us
    pallas_call x1, Pallas kernels: 5.08 us -> 2.25 us  [wide_shards(): pl.pallas_call(functools.partial(finish_kernel, blocks, width), grid=(dev...]
where the time goes in v4:
time: 99.8 us; the launch traced here: 99.6 us
  Pallas kernels  92.9 us (93%)
  local copies, waits for them, and re-layouts  5.94 us (6%)
    pallas_call x1, Pallas kernels, wide_shards(): pl.pallas_call(functools.partial(exchange_kernel, devices, groups, rows,...  90.7 us
    unnamed x13, local copies, waits for them, and re-layouts  5.94 us
    pallas_call x1, Pallas kernels, wide_shards(): pl.pallas_call(functools.partial(finish_kernel, blocks, width), grid=(dev...  2.25 us

profile of v4, /device:TPU:0, one launch (start us, length us, event | category | flops | bytes accessed | tf_op | source)
XLA Modules:
  0.0 99.6 jit_solution(2651862141857029364)
XLA Ops:
  0.6 0.0 copy-start
  0.6 0.0 copy-start.1
  0.7 0.0 copy-start.2
  0.7 0.0 copy-start.3
  0.7 0.0 copy-start.5
  0.7 90.7 %exchange.1 = (bf16[16,2,128,128]{3,2,1,0:T(8,128)(2,1)}, f32[512,2048]{1,0:T(8,128)}) custom-call(s32[1,128]{1,0:T(1,128)} %bitcast.3, bf16[128,2048]{1,0:T(8,128)(2,1)} %query_ref.1, bf16[128,2048]{1,0:T(8,128)(2,1)} %key_ref.1, bf16[128,2048]{1,0:T(8,128)(2,1)} %value_ref.1, bf16[128,2048]{1,0:T(8,128)(2,1)} %grad_ref.1, ...), custom_call_target="tpu_custom_call" | custom-call | tf_op jit(solution)/shard_map/exchange/pallas_call | solution.py:600
  91.4 0.0 copy-done
  91.4 0.0 copy-done.1
  91.4 0.0 copy-done.2
  91.4 0.0 copy-done.3
  91.4 0.0 copy-done.5
  91.4 0.0 copy-start.4
  91.4 1.2 %copy-done.4 = bf16[16,2,128,128]{3,2,1,0:T(8,128)(2,1)S(1)} copy-done((bf16[16,2,128,128]{3,2,1,0:T(8,128)(2,1)S(1)}, bf16[16,2,128,128]{3,2,1,0:T(8,128)(2,1)}, u32[]{:S(2)}) %copy-start.4) | copy-done | bytes 1048600
  92.7 2.3 %finish.1 = (bf16[128,2048]{1,0:T(8,128)(2,1)}, bf16[128,2048]{1,0:T(8,128)(2,1)}, bf16[128,2048]{1,0:T(8,128)(2,1)}, bf16[128,2048]{1,0:T(8,128)(2,1)}) custom-call(bf16[128,2048]{1,0:T(8,128)(2,1)S(1)} %copy-done, bf16[128,2048]{1,0:T(8,128)(2,1)S(1)} %copy-done.1, bf16[128,2048]{1,0:T(8,128)(2,1)S(1)} %copy-done.2, bf16[128,2048]{1,0:T(8,128)(2,1)S(1)} %copy-done.3, ...), custom_call_target="tpu_custom_call" | custom-call | tf_op jit(solution)/shard_map/finish/pallas_call | solution.py:650
  94.9 4.7 %copy.18 = f32[2,2,128,2048]{3,2,1,0:T(8,128)} copy(f32[2,2,128,2048]{3,2,1,0:T(8,128)} %bitcast.6) | data formatting | bytes 8388608
Async XLA Ops:
  0.6 90.8 %copy-start = (bf16[128,2048]{1,0:T(8,128)(2,1)S(1)}, bf16[128,2048]{1,0:T(8,128)(2,1)}, u32[]{:S(2)}) copy-start(bf16[128,2048]{1,0:T(8,128)(2,1)} %query_ref.1) | copy-start | bytes 1572868
  0.6 90.8 %copy-start.1 = (bf16[128,2048]{1,0:T(8,128)(2,1)S(1)}, bf16[128,2048]{1,0:T(8,128)(2,1)}, u32[]{:S(2)}) copy-start(bf16[128,2048]{1,0:T(8,128)(2,1)} %key_ref.1) | copy-start | bytes 1572868
  0.7 90.8 %copy-start.2 = (bf16[128,2048]{1,0:T(8,128)(2,1)S(1)}, bf16[128,2048]{1,0:T(8,128)(2,1)}, u32[]{:S(2)}) copy-start(bf16[128,2048]{1,0:T(8,128)(2,1)} %value_ref.1) | copy-start | bytes 1572868
  0.7 90.8 %copy-start.3 = (bf16[128,2048]{1,0:T(8,128)(2,1)S(1)}, bf16[128,2048]{1,0:T(8,128)(2,1)}, u32[]{:S(2)}) copy-start(bf16[128,2048]{1,0:T(8,128)(2,1)} %grad_ref.1) | copy-start | bytes 1572868
  0.7 90.8 %copy-start.5 = (s32[128]{0:T(128)S(1)}, s32[128]{0:T(128)}, u32[]{:S(2)}) copy-start(s32[128]{0:T(128)} %param.16) | copy-start | bytes 1540
  91.4 1.2 %copy-start.4 = (bf16[16,2,128,128]{3,2,1,0:T(8,128)(2,1)S(1)}, bf16[16,2,128,128]{3,2,1,0:T(8,128)(2,1)}, u32[]{:S(2)}) copy-start(bf16[16,2,128,128]{3,2,1,0:T(8,128)(2,1)} %get-tuple-element.11.series_ref) | copy-start | bytes 3145732

commit v5 on v3

--- a/solution.py
+++ b/solution.py
@@ -387,15 +387,23 @@
     for load in loads[:4]:
         load.wait()
     gating = gate_column(gate_ref[...])
-    for to in range(devices):
-        span = slice(to * width, (to + 1) * width)
+
+    def make_signal(to):
+        span = pl.ds(pl.multiple_of(to * width, width), width)
         gated = gating * key_ref[:, span].astype(jnp.float32) * value_ref[:, span].astype(jnp.float32)
         back = query_ref[:, span].astype(jnp.float32) * grad_ref[:, span].astype(jnp.float32)
-        send_signal[to, 0] = gated.astype(jnp.bfloat16)
-        send_signal[to, 1] = back.astype(jnp.bfloat16)
+        return gated.astype(jnp.bfloat16), back.astype(jnp.bfloat16)
+
     pl.semaphore_wait(barrier, devices + groups - 2)
-    start_all(0, send_signal, got_signal)
-    got_signal[me] = send_signal[me]
+
+    def ship_signal(step, _):
+        to = partner_at(step, 1)
+        send_signal[to, 0], send_signal[to, 1] = make_signal(to)
+        remote(0, send_signal, got_signal, me, to).start()
+        return 0
+
+    lax.fori_loop(0, devices - 1, ship_signal, 0)
+    got_signal[me, 0], got_signal[me, 1] = make_signal(me)
 
     for load in loads[4:6]:
         load.wait()
@@ -558,7 +566,10 @@
         queries_out[:, span] = (grad_ref[:, span].astype(jnp.float32) * conv).astype(jnp.bfloat16)
         keys_out[:, span] = (back * value_ref[:, span].astype(jnp.float32)).astype(jnp.bfloat16)
         values_out[:, span] = (back * key_ref[:, span].astype(jnp.float32)).astype(jnp.bfloat16)
-        spectrum_out[:, span] = dot(spread_ref[own_spread], half_ref[block])
+
+    for first in range(0, blocks, 2):
+        halves = jnp.concatenate([half_ref[block] for block in range(first, min(first + 2, blocks))], axis=1)
+        spectrum_out[:, first * width : first * width + halves.shape[1]] = dot(spread_ref[own_spread], halves)
 
 
 def wide_shards(query_series, key_series, value_series, grad_out, gate_mask, filter_spectrum):
@@ -620,7 +631,7 @@
         jnp.asarray(back_table),
         jnp.asarray(unmix_table),
     )
-    blocks = 2
+    blocks = math.gcd(devices, 4)
     columns = pl.BlockSpec((rows, blocks * width), lambda step: (0, step))
     mixer_out, queries, keys, values, spectrum = pl.pallas_call(
         functools.partial(finish_kernel, blocks, width),

time: 98.3 us -> 97.6 us (level)
    pallas_call x1, Pallas kernels: 5.08 us -> 3.48 us  [wide_shards(): pl.pallas_call(functools.partial(finish_kernel, blocks, width), grid=(dev...]
where the time goes in v5:
time: 97.6 us; the launch traced here: 97.3 us
  Pallas kernels  94.1 us (96%)
  local copies, waits for them, and re-layouts  2.47 us (3%)
    pallas_call x1, Pallas kernels, wide_shards(): pl.pallas_call(functools.partial(exchange_kernel, devices, groups, rows,...  90.6 us
    pallas_call x1, Pallas kernels, wide_shards(): pl.pallas_call(functools.partial(finish_kernel, blocks, width), grid=(dev...  3.48 us
    unnamed x16, local copies, waits for them, and re-layouts  2.47 us

profile of v5, /device:TPU:0, one launch (start us, length us, event | category | flops | bytes accessed | tf_op | source)
XLA Modules:
  0.0 97.3 jit_solution(14161870047664654258)
XLA Ops:
  0.6 0.0 copy-start
  0.6 0.0 copy-start.1
  0.7 0.0 copy-start.2
  0.7 0.0 copy-start.3
  0.7 0.0 copy-start.6
  0.7 0.0 copy-start.7
  0.7 90.6 %exchange.1 = (bf16[16,256,128]{2,1,0:T(8,128)(2,1)}, bf16[16,2,128,128]{3,2,1,0:T(8,128)(2,1)}) custom-call(s32[1,128]{1,0:T(1,128)} %bitcast.3, bf16[128,2048]{1,0:T(8,128)(2,1)} %query_ref.1, bf16[128,2048]{1,0:T(8,128)(2,1)} %key_ref.1, bf16[128,2048]{1,0:T(8,128)(2,1)} %value_ref.1, bf16[128,2048]{1,0:T(8,128)(2,1)} %grad_ref.1, ...), custom_call_target="tpu_custom_call" | custom-call | tf_op jit(solution)/shard_map/exchange/pallas_call | solution.py:589
  91.3 0.0 copy-done
  91.4 0.0 copy-done.1
  91.4 0.0 copy-done.2
  91.4 0.0 copy-done.3
  91.4 0.0 copy-done.6
  91.4 0.0 copy-done.7
  91.4 0.0 copy-start.4
  91.4 1.2 %copy-done.4 = bf16[16,256,128]{2,1,0:T(8,128)(2,1)S(1)} copy-done((bf16[16,256,128]{2,1,0:T(8,128)(2,1)S(1)}, bf16[16,256,128]{2,1,0:T(8,128)(2,1)}, u32[]{:S(2)}) %copy-start.4) | copy-done | bytes 1048600
  92.6 0.0 copy-start.5
  92.6 1.2 %copy-done.5 = bf16[16,2,128,128]{3,2,1,0:T(8,128)(2,1)S(1)} copy-done((bf16[16,2,128,128]{3,2,1,0:T(8,128)(2,1)S(1)}, bf16[16,2,128,128]{3,2,1,0:T(8,128)(2,1)}, u32[]{:S(2)}) %copy-start.5) | copy-done | bytes 1048600
  93.9 3.5 %finish.1 = (bf16[128,2048]{1,0:T(8,128)(2,1)}, bf16[128,2048]{1,0:T(8,128)(2,1)}, bf16[128,2048]{1,0:T(8,128)(2,1)}, bf16[128,2048]{1,0:T(8,128)(2,1)}, f32[512,2048]{1,0:T(8,128)}) custom-call(bf16[128,2048]{1,0:T(8,128)(2,1)S(1)} %copy-done, bf16[128,2048]{1,0:T(8,128)(2,1)S(1)} %copy-done.1, bf16[128,2048]{1,0:T(8,128)(2,1)S(1)} %copy-done.2, ...), custom_call_target="tpu_custom_call" | custom-call | tf_op jit(solution)/shard_map/finish/pallas_call | solution.py:636
Async XLA Ops:
  0.6 90.7 %copy-start = (bf16[128,2048]{1,0:T(8,128)(2,1)S(1)}, bf16[128,2048]{1,0:T(8,128)(2,1)}, u32[]{:S(2)}) copy-start(bf16[128,2048]{1,0:T(8,128)(2,1)} %query_ref.1) | copy-start | bytes 1572868
  0.6 90.7 %copy-start.1 = (bf16[128,2048]{1,0:T(8,128)(2,1)S(1)}, bf16[128,2048]{1,0:T(8,128)(2,1)}, u32[]{:S(2)}) copy-start(bf16[128,2048]{1,0:T(8,128)(2,1)} %key_ref.1) | copy-start | bytes 1572868
  0.7 90.7 %copy-start.2 = (bf16[128,2048]{1,0:T(8,128)(2,1)S(1)}, bf16[128,2048]{1,0:T(8,128)(2,1)}, u32[]{:S(2)}) copy-start(bf16[128,2048]{1,0:T(8,128)(2,1)} %value_ref.1) | copy-start | bytes 1572868
  0.7 90.7 %copy-start.3 = (bf16[128,2048]{1,0:T(8,128)(2,1)S(1)}, bf16[128,2048]{1,0:T(8,128)(2,1)}, u32[]{:S(2)}) copy-start(bf16[128,2048]{1,0:T(8,128)(2,1)} %grad_ref.1) | copy-start | bytes 1572868
  0.7 90.7 %copy-start.6 = (bf16[2,512,256]{2,1,0:T(8,128)(2,1)S(1)}, bf16[2,512,256]{2,1,0:T(8,128)(2,1)}, u32[]{:S(2)}) copy-start(bf16[2,512,256]{2,1,0:T(8,128)(2,1)} %constant.17.clone.spread_ref) | copy-start | bytes 1572868
  0.7 90.7 %copy-start.7 = (s32[128]{0:T(128)S(1)}, s32[128]{0:T(128)}, u32[]{:S(2)}) copy-start(s32[128]{0:T(128)} %param.16) | copy-start | bytes 1540
  91.4 1.2 %copy-start.4 = (bf16[16,256,128]{2,1,0:T(8,128)(2,1)S(1)}, bf16[16,256,128]{2,1,0:T(8,128)(2,1)}, u32[]{:S(2)}) copy-start(bf16[16,256,128]{2,1,0:T(8,128)(2,1)} %get-tuple-element.12.half_ref) | copy-start | bytes 3145732
  92.6 1.2 %copy-start.5 = (bf16[16,2,128,128]{3,2,1,0:T(8,128)(2,1)S(1)}, bf16[16,2,128,128]{3,2,1,0:T(8,128)(2,1)}, u32[]{:S(2)}) copy-start(bf16[16,2,128,128]{3,2,1,0:T(8,128)(2,1)} %get-tuple-element.13.series_ref) | copy-start | bytes 3145732

commit v6 on v5

--- a/solution.py
+++ b/solution.py
@@ -649,7 +649,7 @@
             pl.BlockSpec((blocks, 2, rows, width), lambda step: (step, 0, 0, 0)),
         ],
         out_specs=(columns,) * 4 + (pl.BlockSpec((4 * rows, blocks * width), lambda step: (0, step)),),
-        compiler_params=pltpu.CompilerParams(vmem_limit_bytes=32 * 1024 * 1024),
+        compiler_params=pltpu.CompilerParams(vmem_limit_bytes=60 * 1024 * 1024),
         name="finish",
     )(query_series, key_series, value_series, grad_out, gating, jnp.asarray(spreads), got_grad, got_series)
     return mixer_out, queries, keys, values, spectrum.reshape(2, 2, rows, channels)

time: 97.6 us -> 96.5 us (0.989)
  local copies, waits for them, and re-layouts: 2.47 us -> 0 us
  Pallas kernels: 94.1 us -> 95.7 us
    pallas_call x1, Pallas kernels: 3.48 us -> 6.21 us  [wide_shards(): pl.pallas_call(functools.partial(finish_kernel, blocks, width), grid=(dev...]
    unnamed x16 -> x0, local copies, waits for them, and re-layouts: 2.47 us -> none
    pallas_call x1, Pallas kernels: 90.6 us -> 89.4 us  [wide_shards(): pl.pallas_call(functools.partial(exchange_kernel, devices, groups, rows,...]
where the time goes in v6:
time: 96.5 us; the launch traced here: 96.3 us
  Pallas kernels  95.7 us (99%)
    pallas_call x1, Pallas kernels, wide_shards(): pl.pallas_call(functools.partial(exchange_kernel, devices, groups, rows,...  89.4 us
    pallas_call x1, Pallas kernels, wide_shards(): pl.pallas_call(functools.partial(finish_kernel, blocks, width), grid=(dev...  6.21 us

profile of v6, /device:TPU:0, one launch (start us, length us, event | category | flops | bytes accessed | tf_op | source)
XLA Modules:
  0.0 96.3 jit_solution(17015267202440574400)
XLA Ops:
  0.6 89.4 %exchange.1 = (bf16[16,256,128]{2,1,0:T(8,128)(2,1)}, bf16[16,2,128,128]{3,2,1,0:T(8,128)(2,1)}) custom-call(s32[1,128]{1,0:T(1,128)} %bitcast.4, bf16[128,2048]{1,0:T(8,128)(2,1)} %query_ref.1, bf16[128,2048]{1,0:T(8,128)(2,1)} %key_ref.1, bf16[128,2048]{1,0:T(8,128)(2,1)} %value_ref.1, bf16[128,2048]{1,0:T(8,128)(2,1)} %grad_ref.1, ...), custom_call_target="tpu_custom_call" | custom-call | tf_op jit(solution)/shard_map/exchange/pallas_call | solution.py:589
  90.1 6.2 %finish.1 = (bf16[128,2048]{1,0:T(8,128)(2,1)}, bf16[128,2048]{1,0:T(8,128)(2,1)}, bf16[128,2048]{1,0:T(8,128)(2,1)}, bf16[128,2048]{1,0:T(8,128)(2,1)}, f32[512,2048]{1,0:T(8,128)}) custom-call(bf16[128,2048]{1,0:T(8,128)(2,1)} %query_ref.1, bf16[128,2048]{1,0:T(8,128)(2,1)} %key_ref.1, bf16[128,2048]{1,0:T(8,128)(2,1)} %value_ref.1, ...), custom_call_target="tpu_custom_call" | custom-call | tf_op jit(solution)/shard_map/finish/pallas_call | solution.py:636
